TPU v7x, 512 devices: a whole 4x8x8 slice. The times are simulated.
512 devices in a mesh: rows: 64 (over z, y_hi, core), cols: 8 (over y_lo, x).
Axes of the slice: x: 4, y: 8 (y_hi: 4, y_lo: 2; y = y_hi * 2 + y_lo), z: 8, core: 2. Of those that a mesh axis runs over, the one named last changes fastest.
Arguments:
- momentum: bfloat16 [25600, 2816], P('rows', 'cols'), may hold values from -6 to 6
Outputs:
- iterate: bfloat16 [25600, 2816], P('rows', 'cols')
All inputs are finite; a program needn't handle non-finite values.
Results may differ from a plain program's by a relative error of at most 0.01.
Values may be sent and summed in bfloat16 or wider, within the bound.
A program may use at most 64 MiB of HBM per device.

v0:
```python
import jax
import jax.numpy as jnp
from jax import lax
from jax.sharding import PartitionSpec as P

ROWS = 25600


coef_a = 3.4445
coef_b = -4.775
coef_c = 2.0315


def local(momentum):
    full_rows = lax.all_gather(momentum, "cols", axis=1, tiled=True)
    partial_value = (
        lax.dot_general(
            momentum, full_rows, (((0,), (0,)), ((), ())), preferred_element_type=jnp.float32
        )
        / ROWS
    )
    gram_tile = lax.psum_scatter(partial_value, "rows", scatter_dimension=1, tiled=True).astype(
        jnp.bfloat16
    )
    gram_strip = lax.all_gather(gram_tile, "rows", axis=1, tiled=True)
    left = gram_strip
    square = jnp.dot(
        left,
        lax.all_gather(gram_tile, "cols", axis=0, tiled=True),
        preferred_element_type=jnp.float32,
    )
    poly_tile = (coef_b * gram_tile.astype(jnp.float32) + coef_c * square).astype(jnp.bfloat16)
    left = full_rows
    update = lax.dot_general(
        left,
        lax.all_gather(poly_tile, "rows", axis=1, tiled=True),
        (((1,), (1,)), ((), ())),
        preferred_element_type=jnp.float32,
    )
    return (coef_a * momentum.astype(jnp.float32) + update).astype(jnp.bfloat16)


def solution(mesh):
    return jax.shard_map(
        local,
        mesh=mesh,
        in_specs=(P("rows", "cols"),),
        out_specs=P("rows", "cols"),
        check_vma=False,
    )
```

profile of v0, /device:TPU:1, one launch (start us, length us, event | category | flops | bytes accessed | tf_op | source)
XLA Modules:
  0.0 458.6 jit_solution(17141498574195459565)
XLA Ops:
  6.5 0.7 all-gather.8.cloned.1.call-update
  7.3 0.0 all-gather.10.cloned.1.call-start
  7.3 50.8 %all-gather.8.cloned.1.call-done = bf16[8,352,400]{1,2,0:T(8,128)(2,1)} async-done(((bf16[1,352,400]{1,2,0:T(8,128)(2,1)}), bf16[8,352,400]{1,2,0:T(8,128)(2,1)}) %all-gather.8.cloned.1.call-update) | async-done | bytes 2252816 | tf_op jit(solution)/shard_map/all_gather | solution.py:15
  58.1 2.2 copy.4
  60.4 0.0 copy-start.1
  60.4 3.2 reshape.1
  63.6 5.4 %convolution_multiply_fusion = f32[352,2816]{0,1:T(8,128)} fusion(bf16[400,352]{1,0:T(8,128)(2,1)S(1)} %copy-done.1, bf16[2816,400]{0,1:T(8,128)(2,1)} %reshape.1), kind=kOutput, calls=%fused_computation | convolution fusion | flops 793976832 | bytes 6499328 | tf_op jit(solution)/shard_map/dot_general | solution.py:17
  69.0 167.4 %fusion = f32[352,48]{0,1:T(8,128)S(1)} fusion(f32[352,2816]{0,1:T(8,128)} %convolution_multiply_fusion), kind=kCustom, calls=%all-reduce-scatter | all-reduce-scatter fusion | flops 1081345 | bytes 4034560
  236.4 1.3 collective-permute-start.5
  237.7 1.3 collective-permute-start.1
  239.0 1.3 collective-permute-start.2
  240.3 1.3 collective-permute-start.3
  241.6 1.3 collective-permute-start.4
  243.0 4.6 %collective-permute-start = (bf16[352,48]{0,1:T(8,128)(2,1)S(1)}, bf16[352,48]{0,1:T(8,128)(2,1)S(1)}, u32[]{:S(2)}, u32[]{:S(2)}) collective-permute-start(bf16[352,48]{0,1:T(8,128)(2,1)S(1)} %convert.10), channel_id=1, source_target_pairs={{0,8},{8,16},{16,24},{24,32},{32,40},{40,48},{48,56},{56,64},{64,7... | collective-permute-start | bytes 101384
  247.6 1.3 dynamic-slice.4
  249.5 0.0 collective-permute-done.2
  249.5 0.0 collective-permute-done.3
  249.5 2.0 collective-permute-done
  251.5 1.3 concatenate
  252.9 0.6 fusion.6
  253.5 0.0 all-gather.10.cloned.1.call-update
  253.5 0.0 all-gather.12.cloned.1.call-start
  253.6 28.6 %all-gather.2 = bf16[8,352,44]{1,2,0:T(8,128)(2,1)S(1)} all-gather(bf16[1,352,44]{1,2,0:T(8,128)(2,1)S(1)} %fusion.5), channel_id=1, replica_groups=mesh['rows'=64,'cols'=8] {'cols'}, dimensions={0}, use_global_device_ids=true | all-gather | bytes 278784 | tf_op jit(solution)/shard_map/all_gather | solution.py:29
  282.2 0.1 copy.5
  282.3 0.3 reshape.5
  282.6 76.8 %all-gather.10.cloned.1.call-done = bf16[64,44,352]{2,1,0:T(8,128)(2,1)} async-done(((bf16[1,44,352]{2,1,0:T(8,128)(2,1)}), bf16[64,44,352]{2,1,0:T(8,128)(2,1)}) %all-gather.10.cloned.1.call-update) | async-done | bytes 1982480 | tf_op jit(solution)/shard_map/all_gather | solution.py:25
  359.4 2.8 reshape.3
  362.2 1.0 fusion.3
  363.2 0.0 all-gather.12.cloned.1.call-update
  363.3 81.0 %all-gather.12.cloned.1.call-done = bf16[64,44,352]{2,1,0:T(8,128)(2,1)} async-done(((bf16[1,44,352]{2,1,0:T(8,128)(2,1)}), bf16[64,44,352]{2,1,0:T(8,128)(2,1)}) %all-gather.12.cloned.1.call-update) | async-done | bytes 1982480 | tf_op jit(solution)/shard_map/all_gather | solution.py:36
  444.2 4.2 reshape.7
  448.4 3.7 fusion.2
  (10 shorter events, 0.1 us)
Async XLA Ops:
  6.5 51.6 %all-gather.8.cloned.1.call-start = ((), (), s32[]{:S(2)}) async-start(), calls=%async_computation | async-start | bytes 2764800 | tf_op jit(solution)/shard_map/all_gather | solution.py:15
  7.3 352.1 %all-gather.10.cloned.1.call-start = ((), (), s32[]{:S(2)}) async-start(), calls=%async_computation.1 | async-start | bytes 2396160 | tf_op jit(solution)/shard_map/all_gather | solution.py:25
  60.4 3.2 copy-start.1
  236.4 6.5 %collective-permute-start.5 = (bf16[352,12]{0,1:T(8,128)(2,1)S(1)}, bf16[352,12]{0,1:T(8,128)(2,1)S(1)}, u32[]{:S(2)}, u32[]{:S(2)}) collective-permute-start(bf16[352,12]{0,1:T(8,128)(2,1)S(1)} %slice), channel_id=1, source_target_pairs={{0,48},{8,56},{16,64},{24,72},{32,80},{40,88},{48,96},{56,104},{64... | collective-permute-start | bytes 25352
  237.7 11.7 %collective-permute-start.1 = (bf16[352,48]{0,1:T(8,128)(2,1)S(1)}, bf16[352,48]{0,1:T(8,128)(2,1)S(1)}, u32[]{:S(2)}, u32[]{:S(2)}) collective-permute-start(bf16[352,48]{0,1:T(8,128)(2,1)S(1)} %convert.10), channel_id=1, source_target_pairs={{0,16},{8,24},{16,32},{24,40},{32,48},{40,56},{48,64},{56,72},{64,... | collective-permute-start | bytes 101384
  239.0 10.4 %collective-permute-start.2 = (bf16[352,48]{0,1:T(8,128)(2,1)S(1)}, bf16[352,48]{0,1:T(8,128)(2,1)S(1)}, u32[]{:S(2)}, u32[]{:S(2)}) collective-permute-start(bf16[352,48]{0,1:T(8,128)(2,1)S(1)} %convert.10), channel_id=1, source_target_pairs={{0,24},{8,32},{16,40},{24,48},{32,56},{40,64},{48,72},{56,80},{64,... | collective-permute-start | bytes 101384
  240.3 9.2 %collective-permute-start.3 = (bf16[352,48]{0,1:T(8,128)(2,1)S(1)}, bf16[352,48]{0,1:T(8,128)(2,1)S(1)}, u32[]{:S(2)}, u32[]{:S(2)}) collective-permute-start(bf16[352,48]{0,1:T(8,128)(2,1)S(1)} %convert.10), channel_id=1, source_target_pairs={{0,32},{8,40},{16,48},{24,56},{32,64},{40,72},{48,80},{56,88},{64,... | collective-permute-start | bytes 101384
  241.6 7.9 %collective-permute-start.4 = (bf16[352,48]{0,1:T(8,128)(2,1)S(1)}, bf16[352,48]{0,1:T(8,128)(2,1)S(1)}, u32[]{:S(2)}, u32[]{:S(2)}) collective-permute-start(bf16[352,48]{0,1:T(8,128)(2,1)S(1)} %convert.10), channel_id=1, source_target_pairs={{0,40},{8,48},{16,56},{24,64},{32,72},{40,80},{48,88},{56,96},{64,... | collective-permute-start | bytes 101384
  243.0 8.6 %collective-permute-start = (bf16[352,48]{0,1:T(8,128)(2,1)S(1)}, bf16[352,48]{0,1:T(8,128)(2,1)S(1)}, u32[]{:S(2)}, u32[]{:S(2)}) collective-permute-start(bf16[352,48]{0,1:T(8,128)(2,1)S(1)} %convert.10), channel_id=1, source_target_pairs={{0,8},{8,16},{16,24},{24,32},{32,40},{40,48},{48,56},{56,64},{64,7... | collective-permute-start | bytes 101384
  253.5 190.7 %all-gather.12.cloned.1.call-start = ((), (), s32[]{:S(2)}) async-start(), calls=%async_computation.2 | async-start | bytes 2396160 | tf_op jit(solution)/shard_map/all_gather | solution.py:36
  363.2 85.1 %copy-start = (bf16[2816,400]{0,1:T(8,128)(2,1)S(1)}, bf16[2816,400]{0,1:T(8,128)(2,1)}, u32[]{:S(2)}) copy-start(bf16[2816,400]{0,1:T(8,128)(2,1)} %reshape.1) | copy-start | bytes 6758404
Sparse Core Ops, SparseCore 0:
  9.4 48.6 all-gather.7
  253.6 105.6 all-gather.9
  363.4 80.7 all-gather.11
where the time goes:
time: 459 us
  waiting for transfers between devices  211 us (46%)
  blocking collectives  196 us (43%)
  local copies, waits for them, and re-layouts  16 us (3%)
  between operations  13.9 us (3%)
  starting transfers between devices  11.1 us (2%)
  matrix products  10.1 us (2%)
    unnamed x1, blocking collectives  167 us
    all_gather x1, waiting for transfers between devices, local(): lax.all_gather(poly_tile, 'rows', axis=1, tiled=True)  81 us
    all_gather x1, waiting for transfers between devices, local(): gram_strip = lax.all_gather(gram_tile, 'rows', axis=1, tiled=True)  76.8 us
    all_gather x1, waiting for transfers between devices, local(): full_rows = lax.all_gather(momentum, 'cols', axis=1, tiled=True)  50.8 us
    all_gather x1, blocking collectives, local(): lax.all_gather(gram_tile, 'cols', axis=0, tiled=True)  28.6 us
    unnamed x13, local copies, waits for them, and re-layouts  13.7 us
    unnamed x6, starting transfers between devices  11 us
  transfers between devices with their start and end apart: 9, of which 4 were waited for; matrix products, arithmetic and copies ran while one was open for 0% of the time, Pallas kernels for 0%

commit v1 on v0

v1 whole, which is shorter than its diff:
```python
import jax
import jax.numpy as jnp
from jax import lax
from jax.experimental import pallas as pl
from jax.experimental.pallas import tpu as pltpu
from jax.sharding import PartitionSpec as P

ROWS = 25600

coef_a = 3.4445
coef_b = -4.775
coef_c = 2.0315

NZ, NY, NX = 8, 4, 4
NB = 8
MESH = pl.DeviceIdType.MESH
F32, BF16 = jnp.float32, jnp.bfloat16


def kernel(
    x_hbm, o_ref, xx, sb, rb, yb, gl, gr, pf, lt,
    loc, xs, xr, cs, cr, zs, zr, ys, yr, gzs, gzr, gxs, gxr, gcs, gcr, pzs, pzr, pcs, pcr,
):
    m, w = x_hbm.shape
    h = w // 2
    r, c = lax.axis_index("rows"), lax.axis_index("cols")
    z, yh, k = r // (NY * 2), lax.rem(r // 2, NY), lax.rem(r, 2)
    yl, x = c // NX, lax.rem(c, NX)

    def rid(z=z, yh=yh, k=k):
        return (z * NY + yh) * 2 + k

    def cid(yl=yl, x=x):
        return yl * NX + x

    def at_x(d):
        return lax.rem(x + d, NX)

    def at_z(d):
        return lax.rem(z + d, NZ)

    def at_y(d):
        return lax.rem(yh + d, NY)

    sends = []

    def send(src, dst, ss, rs, to):
        copy = pltpu.make_async_remote_copy(
            src_ref=src, dst_ref=dst, send_sem=ss, recv_sem=rs, device_id=to, device_id_type=MESH
        )
        copy.start()
        sends.append(copy)

    def arrived(dst, ss, rs):
        pltpu.make_async_remote_copy(
            src_ref=dst, dst_ref=dst, send_sem=ss, recv_sem=rs, device_id=core, device_id_type=MESH
        ).wait_recv()

    core = (rid(k=1 - k), c)
    ypair = (r, cid(yl=1 - yl))
    xdev = [(r, cid(x=at_x(d))) for d in range(NX)]
    zdev = [(rid(z=at_z(d)), c) for d in range(NZ)]
    ydev = [(rid(yh=at_y(d)), c) for d in range(NY)]

    mine = xx.at[c, pl.ds(k * m, m)]
    own = pltpu.make_async_copy(x_hbm, mine, loc)
    own.start()

    barrier = pltpu.get_barrier_semaphore()
    partners = [core, ypair] + xdev[1:] + zdev[1:] + ydev[1:]
    for to in partners:
        pl.semaphore_signal(barrier, inc=1, device_id=to, device_id_type=MESH)
    pl.semaphore_wait(barrier, len(partners))
    own.wait()

    def half(b):
        return xx.at[b, pl.ds(k * m, m)]

    def other(b):
        return xx.at[b, pl.ds((1 - k) * m, m)]

    send(mine, mine, xs.at[0], xr.at[c], ypair)
    for i, d in enumerate((1, 3, 2)):
        send(mine, mine, xs.at[1 + i], xr.at[c], xdev[d])
    send(mine, mine, cs.at[0], cr.at[c], core)

    c2 = cid(yl=1 - yl)
    order = [c, c2] + [cid(x=at_x(d)) for d in (1, 3, 2)] + [cid(yl=1 - yl, x=at_x(d)) for d in (1, 3, 2)]
    pick = (
        lax.broadcasted_iota(jnp.int32, (h, w), 1) == lax.broadcasted_iota(jnp.int32, (h, w), 0) + k * h
    ).astype(BF16)
    for i, b in enumerate(order):
        if i > 0:
            arrived(half(b), xs.at[0], xr.at[b])
            if i == 1:
                for j, d in enumerate((1, 3, 2)):
                    send(half(b), half(b), xs.at[4 + j], xr.at[b], xdev[d])
            send(half(b), half(b), cs.at[i], cr.at[b], core)
        arrived(other(b), xs.at[0], cr.at[b])
        if i == 0:
            lt[...] = lax.dot_general(
                pick, xx[c], (((1,), (1,)), ((), ())), preferred_element_type=F32
            ).astype(BF16)
        sb[i] = jnp.dot(lt[...], xx[b], preferred_element_type=F32).astype(BF16)

        @pl.when(b != z)
        def _():
            pltpu.make_async_remote_copy(
                src_ref=sb.at[i], dst_ref=rb.at[z], send_sem=zs.at[i], recv_sem=zr.at[z],
                device_id=(rid(z=b), c), device_id_type=MESH,
            ).start()

        @pl.when(b == z)
        def _():
            rb[z] = sb[i]

    for d in range(1, NZ):
        s = at_z(d)
        arrived(rb.at[s], zs.at[0], zr.at[s])
    part = rb[0].astype(F32)
    for s in range(1, NZ):
        part = part + rb[s].astype(F32)
    yb[yh] = part.astype(BF16)
    for d in (1, 3, 2):
        send(yb.at[yh], yb.at[yh], ys.at[d], yr.at[yh], ydev[d])
    for d in (1, 3, 2):
        s = at_y(d)
        arrived(yb.at[s], ys.at[0], yr.at[s])
    total = yb[0].astype(F32)
    for s in range(1, NY):
        total = total + yb[s].astype(F32)
    gram = (total / ROWS).astype(BF16)
    top = pl.ds(k * h, h)
    low = pl.ds((1 - k) * h, h)
    gl[z] = gram
    gr[c, top, :] = gram

    g0 = gr.at[c, top]
    send(gl.at[z], gl.at[z], gzs.at[0], gzr.at[z], zdev[1])
    send(gl.at[z], gl.at[z], gzs.at[4], gzr.at[z], zdev[7])
    send(g0, g0, gxs.at[0], gxr.at[c], ypair)
    for i, d in enumerate((1, 3, 2)):
        send(g0, g0, gxs.at[1 + i], gxr.at[c], xdev[d])
    send(g0, g0, gcs.at[0], gcr.at[c], core)

    def ring(buf, ss, rs, step):
        right, left = at_z(NZ - 1 - step), at_z(1 + step)
        arrived(buf(right), ss.at[0], rs.at[right])
        if step < 3:
            send(buf(right), buf(right), ss.at[1 + step], rs.at[right], zdev[1])
        if step < 3:
            arrived(buf(left), ss.at[0], rs.at[left])
            if step < 2:
                send(buf(left), buf(left), ss.at[5 + step], rs.at[left], zdev[7])
            return [right, left]
        return [right]

    def column(i):
        b = order[i]
        g = gr.at[b, top]
        arrived(g, gxs.at[0], gxr.at[b])
        if i == 1:
            for j, d in enumerate((1, 3, 2)):
                send(g, g, gxs.at[4 + j], gxr.at[b], xdev[d])
        send(g, g, gcs.at[i], gcr.at[b], core)

    column(1)
    for step in range(4):
        ring(lambda s: gl.at[s], gzs, gzr, step)
        if step < 3:
            column(2 + 2 * step)
            column(3 + 2 * step)
    for b in order:
        g = gr.at[b, low]
        arrived(g, gcs.at[0], gcr.at[b])
    square = jnp.dot(gl[0], gr[0], preferred_element_type=F32)
    for s in range(1, NB):
        square = square + jnp.dot(gl[s], gr[s], preferred_element_type=F32)
    pf[z, top, :] = (coef_b * gram.astype(F32) + coef_c * square).astype(BF16)

    def poly(s):
        return pf.at[s, top]

    send(poly(z), poly(z), pzs.at[0], pzr.at[z], zdev[1])
    send(poly(z), poly(z), pzs.at[4], pzr.at[z], zdev[7])
    send(poly(z), poly(z), pcs.at[0], pcr.at[z], core)

    def term(s):
        arrived(pf.at[s, low], pcs.at[0], pcr.at[s])
        return lax.dot_general(
            xx[s, pl.ds(k * m, m)], pf[s], (((1,), (1,)), ((), ())), preferred_element_type=F32
        )

    update = term(z)
    n = 1
    for step in range(4):
        got = ring(poly, pzs, pzr, step)
        for s in got:
            send(poly(s), poly(s), pcs.at[n], pcr.at[s], core)
            n += 1
        for s in got:
            update = update + term(s)
    o_ref[...] = (coef_a * xx[c, pl.ds(k * m, m)].astype(F32) + update).astype(BF16)

    for copy in sends:
        copy.wait_send()
    for i, b in enumerate(order):

        @pl.when(b != z)
        def _():
            pltpu.make_async_remote_copy(
                src_ref=sb.at[i], dst_ref=rb.at[z], send_sem=zs.at[i], recv_sem=zr.at[z],
                device_id=core, device_id_type=MESH,
            ).wait_send()


def local(momentum):
    m, w = momentum.shape
    h = w // 2
    dma = lambda n: pltpu.SemaphoreType.DMA((n,))
    return pl.pallas_call(
        kernel,
        out_shape=jax.ShapeDtypeStruct((m, w), BF16),
        in_specs=[pl.BlockSpec(memory_space=pl.ANY)],
        out_specs=pl.BlockSpec(memory_space=pltpu.VMEM),
        scratch_shapes=[
            pltpu.VMEM((NB, 2 * m, w), BF16),
            pltpu.VMEM((NB, h, w), BF16),
            pltpu.VMEM((NZ, h, w), BF16),
            pltpu.VMEM((NY, h, w), BF16),
            pltpu.VMEM((NZ, h, w), BF16),
            pltpu.VMEM((NB, w, w), BF16),
            pltpu.VMEM((NZ, w, w), BF16),
            pltpu.VMEM((h, 2 * m), BF16),
            pltpu.SemaphoreType.DMA,
            dma(7), dma(8), dma(8), dma(8),
            dma(8), dma(8), dma(4), dma(4),
            dma(7), dma(8), dma(7), dma(8), dma(8), dma(8),
            dma(7), dma(8), dma(8), dma(8),
        ],
        compiler_params=pltpu.CompilerParams(
            collective_id=0, has_side_effects=True, vmem_limit_bytes=48 << 20
        ),
        name="newton_schulz",
    )(momentum)


def solution(mesh):
    return jax.shard_map(
        local,
        mesh=mesh,
        in_specs=(P("rows", "cols"),),
        out_specs=P("rows", "cols"),
        check_vma=False,
    )
```

time: 459 us -> 118 us (0.26)
  waiting for transfers between devices: 211 us -> 0 us
  blocking collectives: 196 us -> 0 us
  Pallas kernels: 0 us -> 116 us
  local copies, waits for them, and re-layouts: 16 us -> 1.69 us
  between operations: 13.9 us -> 0.01 us
  starting transfers between devices: 11.1 us -> 0 us
  matrix products: 10.1 us -> 0 us
    all_gather x3 -> x0, waiting for transfers between devices: 209 us -> none  [the longest x1 81 us: local(): lax.all_gather(poly_tile, 'rows', axis=1, tiled=True)]
    unnamed x1 -> x0, blocking collectives: 167 us -> none
    pallas_call x0 -> x1, Pallas kernels: none -> 116 us  [local(): pl.pallas_call(kernel, out_shape=jax.ShapeDtypeStruct((m, w), BF16), in_s...]
    all_gather x1 -> x0, blocking collectives: 28.6 us -> none  [local(): lax.all_gather(gram_tile, 'cols', axis=0, tiled=True)]
    unnamed x13 -> x3, local copies, waits for them, and re-layouts: 13.7 us -> 1.69 us
    unnamed x6 -> x0, starting transfers between devices: 11 us -> none
    dot_general x3 -> x0, matrix products: 10.1 us -> none  [the longest x1 5.38 us: local(): lax.dot_general(momentum, full_rows, (((0,), (0,)), ((), ())), preferred_...]
  transfers between devices with their start and end apart: 9 -> 0, of which waited for: 4 -> 0; matrix products, arithmetic and copies ran while one was open for 0% -> 0% of each run, Pallas kernels for 0% -> 0%
where the time goes in v1:
time: 118 us
  Pallas kernels  116 us (98%)
  local copies, waits for them, and re-layouts  1.69 us (1%)
    pallas_call x1, Pallas kernels, local(): pl.pallas_call(kernel, out_shape=jax.ShapeDtypeStruct((m, w), BF16), in_s...  116 us

profile of v1, /device:TPU:1, one launch (start us, length us, event | category | flops | bytes accessed | tf_op | source)
XLA Modules:
  0.0 117.9 jit_solution(10681279933755282635)
XLA Ops:
  0.0 0.0 copy-start
  0.0 1.0 copy-done
  1.0 116.2 %newton_schulz.1 = bf16[400,352]{1,0:T(8,128)(2,1)S(1)} custom-call(bf16[400,352]{1,0:T(8,128)(2,1)S(1)} %copy-done), custom_call_target="tpu_custom_call" | custom-call | tf_op jit(solution)/shard_map/newton_schulz/pallas_call | solution.py:221
  117.2 0.7 copy.3
Async XLA Ops:
  0.0 1.0 copy-start

commit v2 on v1

--- a/solution.py
+++ b/solution.py
@@ -19,10 +19,11 @@
 
 def kernel(
     x_hbm, o_ref, xx, sb, rb, yb, gl, gr, pf, lt,
-    loc, xs, xr, cs, cr, zs, zr, ys, yr, gzs, gzr, gxs, gxr, gcs, gcr, pzs, pzr, pcs, pcr,
+    loc, xs, xr, cs, cr, zs, zr, ys, yr, gzs, gzr, gys, gyr, gxs, gxs2, gxr, gcs, gcr, pzs, pzr, pcs, pcr,
 ):
     m, w = x_hbm.shape
     h = w // 2
+    cut = -(-h // 32) * 16
     r, c = lax.axis_index("rows"), lax.axis_index("cols")
     z, yh, k = r // (NY * 2), lax.rem(r // 2, NY), lax.rem(r, 2)
     yl, x = c // NX, lax.rem(c, NX)
@@ -136,40 +137,66 @@
     gr[c, top, :] = gram
 
     g0 = gr.at[c, top]
-    send(gl.at[z], gl.at[z], gzs.at[0], gzr.at[z], zdev[1])
-    send(gl.at[z], gl.at[z], gzs.at[4], gzr.at[z], zdev[7])
-    send(g0, g0, gxs.at[0], gxr.at[c], ypair)
-    for i, d in enumerate((1, 3, 2)):
-        send(g0, g0, gxs.at[1 + i], gxr.at[c], xdev[d])
-    send(g0, g0, gcs.at[0], gcr.at[c], core)
-
-    def ring(buf, ss, rs, step):
-        right, left = at_z(NZ - 1 - step), at_z(1 + step)
-        arrived(buf(right), ss.at[0], rs.at[right])
-        if step < 3:
-            send(buf(right), buf(right), ss.at[1 + step], rs.at[right], zdev[1])
-        if step < 3:
-            arrived(buf(left), ss.at[0], rs.at[left])
-            if step < 2:
-                send(buf(left), buf(left), ss.at[5 + step], rs.at[left], zdev[7])
-            return [right, left]
-        return [right]
-
-    def column(i):
-        b = order[i]
-        g = gr.at[b, top]
-        arrived(g, gxs.at[0], gxr.at[b])
-        if i == 1:
-            for j, d in enumerate((1, 3, 2)):
-                send(g, g, gxs.at[4 + j], gxr.at[b], xdev[d])
-        send(g, g, gcs.at[i], gcr.at[b], core)
-
-    column(1)
-    for step in range(4):
-        ring(lambda s: gl.at[s], gzs, gzr, step)
-        if step < 3:
-            column(2 + 2 * step)
-            column(3 + 2 * step)
+    def part_of(n):
+        return pl.ds(0, cut) if n == 0 else pl.ds(cut, h - cut)
+
+    def g_row(s, n):
+        return gl.at[s, part_of(n)]
+
+    def g_col(b, n):
+        return gr.at[b, pl.ds(k * h + n * cut, h - cut if n else cut)]
+
+    def p_row(s, n):
+        return pf.at[s, pl.ds(k * h + n * cut, h - cut if n else cut)]
+
+    def ring_hop(buf, ss, rs, dev, slots, hop, right, n):
+        reach = len(slots) // 2 - (right == n)
+        if hop > reach:
+            return
+        s = slots[-hop if right else hop] if hop else slots[0]
+        if hop:
+            arrived(buf(s, n), ss.at[0, 0, 0], rs.at[s, n])
+        if hop < reach:
+            send(buf(s, n), buf(s, n), ss.at[hop, right, n], rs.at[s, n], dev[1 if right else -1])
+
+    def ring_step(*args):
+        for right, n in ((1, 0), (0, 1), (1, 1), (0, 0)):
+            ring_hop(*args, right, n)
+
+    zslots = [at_z(d) for d in range(NZ)]
+    xslots = [cid(x=at_x(d)) for d in range(NX)]
+    xslots2 = [cid(yl=1 - yl, x=at_x(d)) for d in range(NX)]
+    zring = (g_row, gzs, gzr, zdev, zslots)
+    xring = (g_col, gxs, gxr, xdev, xslots)
+    xring2 = (g_col, gxs2, gxr, xdev, xslots2)
+
+    for n in range(2):
+        send(g_col(c, n), g_col(c, n), gys.at[n], gyr.at[n], ypair)
+    ring_step(*xring, 0)
+    ring_step(*zring, 0)
+    send(gr.at[c, top], gr.at[c, top], gcs.at[0], gcr.at[c], core)
+
+    def hand_on(slots, first, ds):
+        for i, d in enumerate(ds):
+            g = gr.at[slots[d], top]
+            send(g, g, gcs.at[first + i], gcr.at[slots[d]], core)
+
+    for n in range(2):
+        arrived(g_col(c2, n), gys.at[0], gyr.at[n])
+    ring_step(*xring2, 0)
+    hand_on(xslots2, 1, (0,))
+    ring_step(*xring, 1)
+    ring_step(*zring, 1)
+    hand_on(xslots, 2, (1, 3))
+    ring_step(*xring, 2)
+    ring_step(*zring, 2)
+    hand_on(xslots, 4, (2,))
+    ring_step(*xring2, 1)
+    hand_on(xslots2, 5, (1, 3))
+    ring_step(*zring, 3)
+    ring_step(*xring2, 2)
+    hand_on(xslots2, 7, (2,))
+    ring_step(*zring, 4)
     for b in order:
         g = gr.at[b, low]
         arrived(g, gcs.at[0], gcr.at[b])
@@ -177,13 +204,9 @@
     for s in range(1, NB):
         square = square + jnp.dot(gl[s], gr[s], preferred_element_type=F32)
     pf[z, top, :] = (coef_b * gram.astype(F32) + coef_c * square).astype(BF16)
-
-    def poly(s):
-        return pf.at[s, top]
-
-    send(poly(z), poly(z), pzs.at[0], pzr.at[z], zdev[1])
-    send(poly(z), poly(z), pzs.at[4], pzr.at[z], zdev[7])
-    send(poly(z), poly(z), pcs.at[0], pcr.at[z], core)
+    pring = (p_row, pzs, pzr, zdev, zslots)
+    ring_step(*pring, 0)
+    send(pf.at[z, top], pf.at[z, top], pcs.at[0], pcr.at[z], core)
 
     def term(s):
         arrived(pf.at[s, low], pcs.at[0], pcr.at[s])
@@ -193,15 +216,15 @@
 
     update = term(z)
     n = 1
-    for step in range(4):
-        got = ring(poly, pzs, pzr, step)
+    for step in range(1, 5):
+        ring_step(*pring, step)
+        got = [zslots[-step], zslots[step]] if step < 4 else [zslots[4]]
         for s in got:
-            send(poly(s), poly(s), pcs.at[n], pcr.at[s], core)
+            send(pf.at[s, top], pf.at[s, top], pcs.at[n], pcr.at[s], core)
             n += 1
         for s in got:
             update = update + term(s)
     o_ref[...] = (coef_a * xx[c, pl.ds(k * m, m)].astype(F32) + update).astype(BF16)
-
     for copy in sends:
         copy.wait_send()
     for i, b in enumerate(order):
@@ -217,7 +240,7 @@
 def local(momentum):
     m, w = momentum.shape
     h = w // 2
-    dma = lambda n: pltpu.SemaphoreType.DMA((n,))
+    dma = lambda *n: pltpu.SemaphoreType.DMA(n)
     return pl.pallas_call(
         kernel,
         out_shape=jax.ShapeDtypeStruct((m, w), BF16),
@@ -235,8 +258,8 @@
             pltpu.SemaphoreType.DMA,
             dma(7), dma(8), dma(8), dma(8),
             dma(8), dma(8), dma(4), dma(4),
-            dma(7), dma(8), dma(7), dma(8), dma(8), dma(8),
-            dma(7), dma(8), dma(8), dma(8),
+            dma(4, 2, 2), dma(8, 2), dma(2), dma(2), dma(2, 2, 2), dma(2, 2, 2), dma(8, 2), dma(8), dma(8),
+            dma(4, 2, 2), dma(8, 2), dma(8), dma(8),
         ],
         compiler_params=pltpu.CompilerParams(
             collective_id=0, has_side_effects=True, vmem_limit_bytes=48 << 20

time: 118 us -> 117 us (level)
    pallas_call x1, Pallas kernels: 116 us -> 115 us  [local(): pl.pallas_call(kernel, out_shape=jax.ShapeDtypeStruct((m, w), BF16), in_s...]
where the time goes in v2:
time: 117 us
  Pallas kernels  115 us (98%)
  local copies, waits for them, and re-layouts  1.69 us (1%)
    pallas_call x1, Pallas kernels, local(): pl.pallas_call(kernel, out_shape=jax.ShapeDtypeStruct((m, w), BF16), in_s...  115 us

profile of v2, /device:TPU:1, one launch (start us, length us, event | category | flops | bytes accessed | tf_op | source)
XLA Modules:
  0.0 116.5 jit_solution(1202920698843735077)
XLA Ops:
  0.0 0.0 copy-start
  0.0 1.0 copy-done
  1.0 114.8 %newton_schulz.1 = bf16[400,352]{1,0:T(8,128)(2,1)S(1)} custom-call(bf16[400,352]{1,0:T(8,128)(2,1)S(1)} %copy-done), custom_call_target="tpu_custom_call" | custom-call | tf_op jit(solution)/shard_map/newton_schulz/pallas_call | solution.py:244
  115.8 0.7 copy.3
Async XLA Ops:
  0.0 1.0 copy-start

commit v3 on v2

--- a/solution.py
+++ b/solution.py
@@ -13,17 +13,22 @@
 
 NZ, NY, NX = 8, 4, 4
 NB = 8
+EARLY = 4
 MESH = pl.DeviceIdType.MESH
 F32, BF16 = jnp.float32, jnp.bfloat16
 
 
 def kernel(
-    x_hbm, o_ref, xx, sb, rb, yb, gl, gr, pf, lt,
-    loc, xs, xr, cs, cr, zs, zr, ys, yr, gzs, gzr, gys, gyr, gxs, gxs2, gxr, gcs, gcr, pzs, pzr, pcs, pcr,
+    x_hbm, o_ref, xx, sb, rb, eb, yb, qb, zb, tot, gl, gr, pf, lt,
+    loc, ws, wr, xs, xr, xs2, xr2, vys, vyr, cs, cr, zs, zr, zqr, ys, yr, as_, ar, gzs, gzr, gys, gyr, gxs, gxs2, gxr, gcs, gcr, pzs, pzr, pcs, pcr,
 ):
     m, w = x_hbm.shape
     h = w // 2
+    q = qb.shape[1]
+    hp = NY * q
     cut = -(-h // 32) * 16
+    mid = -(-m // 32) * 16
+    qtr = -(-mid // 32) * 16
     r, c = lax.axis_index("rows"), lax.axis_index("cols")
     z, yh, k = r // (NY * 2), lax.rem(r // 2, NY), lax.rem(r, 2)
     yl, x = c // NX, lax.rem(c, NX)
@@ -80,63 +85,15 @@
     def other(b):
         return xx.at[b, pl.ds((1 - k) * m, m)]
 
-    send(mine, mine, xs.at[0], xr.at[c], ypair)
-    for i, d in enumerate((1, 3, 2)):
-        send(mine, mine, xs.at[1 + i], xr.at[c], xdev[d])
-    send(mine, mine, cs.at[0], cr.at[c], core)
-
     c2 = cid(yl=1 - yl)
     order = [c, c2] + [cid(x=at_x(d)) for d in (1, 3, 2)] + [cid(yl=1 - yl, x=at_x(d)) for d in (1, 3, 2)]
-    pick = (
-        lax.broadcasted_iota(jnp.int32, (h, w), 1) == lax.broadcasted_iota(jnp.int32, (h, w), 0) + k * h
-    ).astype(BF16)
-    for i, b in enumerate(order):
-        if i > 0:
-            arrived(half(b), xs.at[0], xr.at[b])
-            if i == 1:
-                for j, d in enumerate((1, 3, 2)):
-                    send(half(b), half(b), xs.at[4 + j], xr.at[b], xdev[d])
-            send(half(b), half(b), cs.at[i], cr.at[b], core)
-        arrived(other(b), xs.at[0], cr.at[b])
-        if i == 0:
-            lt[...] = lax.dot_general(
-                pick, xx[c], (((1,), (1,)), ((), ())), preferred_element_type=F32
-            ).astype(BF16)
-        sb[i] = jnp.dot(lt[...], xx[b], preferred_element_type=F32).astype(BF16)
-
-        @pl.when(b != z)
-        def _():
-            pltpu.make_async_remote_copy(
-                src_ref=sb.at[i], dst_ref=rb.at[z], send_sem=zs.at[i], recv_sem=zr.at[z],
-                device_id=(rid(z=b), c), device_id_type=MESH,
-            ).start()
-
-        @pl.when(b == z)
-        def _():
-            rb[z] = sb[i]
-
-    for d in range(1, NZ):
-        s = at_z(d)
-        arrived(rb.at[s], zs.at[0], zr.at[s])
-    part = rb[0].astype(F32)
-    for s in range(1, NZ):
-        part = part + rb[s].astype(F32)
-    yb[yh] = part.astype(BF16)
-    for d in (1, 3, 2):
-        send(yb.at[yh], yb.at[yh], ys.at[d], yr.at[yh], ydev[d])
-    for d in (1, 3, 2):
-        s = at_y(d)
-        arrived(yb.at[s], ys.at[0], yr.at[s])
-    total = yb[0].astype(F32)
-    for s in range(1, NY):
-        total = total + yb[s].astype(F32)
-    gram = (total / ROWS).astype(BF16)
-    top = pl.ds(k * h, h)
-    low = pl.ds((1 - k) * h, h)
-    gl[z] = gram
-    gr[c, top, :] = gram
-
-    g0 = gr.at[c, top]
+
+    def owner(b):
+        return lax.rem(b, NX) * 2 + b // NX
+
+    def block(s):
+        return s % 2 * NX + s // 2 if isinstance(s, int) else lax.rem(s, 2) * NX + s // 2
+
     def part_of(n):
         return pl.ds(0, cut) if n == 0 else pl.ds(cut, h - cut)
 
@@ -169,6 +126,141 @@
     zring = (g_row, gzs, gzr, zdev, zslots)
     xring = (g_col, gxs, gxr, xdev, xslots)
     xring2 = (g_col, gxs2, gxr, xdev, xslots2)
+
+    def x_half(b, n):
+        return xx.at[b, pl.ds(k * m + n * mid, m - mid if n else mid)]
+
+    def x_quarter(b, n):
+        return xx.at[b, pl.ds(k * m + n * qtr, mid - qtr if n else qtr)]
+
+    def hand(i):
+        send(half(order[i]), half(order[i]), cs.at[i], cr.at[order[i]], core)
+
+    def partial(i):
+        b = order[i]
+        if i:
+            arrived(other(b), cs.at[0], cr.at[b])
+        sb[i] = jnp.dot(lt[...], xx[b], preferred_element_type=F32).astype(BF16)
+        if i < EARLY:
+            to_owner(i, sb.at[i], rb, zr)
+        else:
+            j = i - EARLY
+            yb[j, yh] = sb[i, quarter(yh)]
+            for d in (1, 3, 2):
+                send(sb.at[i, quarter(at_y(d))], yb.at[j, yh], ys.at[j, d], yr.at[j, yh], ydev[d])
+
+    def quarter(p):
+        return pl.ds(pl.multiple_of(p * q, q), q)
+
+    def to_owner(i, src, dst, rs):
+        to = owner(order[i])
+
+        @pl.when(to != z)
+        def _():
+            pltpu.make_async_remote_copy(
+                src_ref=src, dst_ref=dst.at[z], send_sem=zs.at[i], recv_sem=rs.at[z],
+                device_id=(rid(z=to), c), device_id_type=MESH,
+            ).start()
+
+        @pl.when(to == z)
+        def _():
+            dst[z] = src[...]
+
+    def late(i):
+        j = i - EARLY
+        add_up(yb.at[j], lambda s: yr.at[j, s], [at_y(d) for d in (1, 3, 2)], qb.at[j])
+        to_owner(i, qb.at[j], zb, zqr)
+
+    def add_up(buf, rs, others, out):
+        for s in others:
+            arrived(buf.at[s], zs.at[0], rs(s))
+        value = buf[0].astype(F32)
+        for s in range(1, buf.shape[0]):
+            value = value + buf[s].astype(F32)
+        out[...] = value.astype(out.dtype)
+
+    def over(i, d):
+        v = x_half(order[i], 1)
+        send(v, v, vys.at[d - 1], vyr.at[order[i]], ypair)
+
+    def back(i):
+        arrived(x_half(order[i], 1), vys.at[0], vyr.at[order[i]])
+
+    rring = (x_half, xs, xr, xdev, xslots)
+    rring2 = (x_quarter, xs2, xr2, xdev, xslots2)
+    for n in range(2):
+        send(x_half(c, n), x_half(c, n), ws.at[n], wr.at[n], ypair)
+    ring_step(*rring, 0)
+    hand(0)
+    pick = (
+        lax.broadcasted_iota(jnp.int32, (hp, w), 1) == lax.broadcasted_iota(jnp.int32, (hp, w), 0) + k * h
+    ).astype(BF16)
+    arrived(other(c), cs.at[0], cr.at[c])
+    lt[...] = lax.dot_general(
+        pick, xx[c], (((1,), (1,)), ((), ())), preferred_element_type=F32
+    ).astype(BF16)
+    partial(0)
+    for n in range(2):
+        arrived(x_half(c2, n), ws.at[0], wr.at[n])
+    hand(1)
+    ring_step(*rring, 1)
+    over(2, 1)
+    over(3, 3)
+    hand(2)
+    hand(3)
+    ring_step(*rring2, 0)
+    partial(1)
+    partial(2)
+    partial(3)
+    ring_step(*rring, 2)
+    over(4, 2)
+    hand(4)
+    partial(4)
+    ring_step(*rring2, 1)
+    for i in (5, 6):
+        back(i)
+        hand(i)
+    partial(5)
+    partial(6)
+    late(4)
+    ring_step(*rring2, 2)
+    back(7)
+    hand(7)
+    late(5)
+    late(6)
+    partial(7)
+    late(7)
+
+    mine_early = owner(order[0]) == z
+    for i in range(1, EARLY):
+        mine_early = jnp.logical_or(mine_early, owner(order[i]) == z)
+    zothers = [at_z(d) for d in range(1, NZ)]
+
+    @pl.when(mine_early)
+    def _():
+        add_up(rb, lambda s: zr.at[s], zothers, eb)
+        yb[NB - EARLY, yh] = eb[quarter(yh)]
+        for d in (1, 3, 2):
+            pltpu.make_async_remote_copy(
+                src_ref=eb.at[quarter(at_y(d))], dst_ref=yb.at[NB - EARLY, yh], send_sem=ys.at[NB - EARLY, d],
+                recv_sem=yr.at[NB - EARLY, yh], device_id=ydev[d], device_id_type=MESH,
+            ).start()
+        add_up(yb.at[NB - EARLY], lambda s: yr.at[NB - EARLY, s], [at_y(d) for d in (1, 3, 2)], tot)
+
+    @pl.when(jnp.logical_not(mine_early))
+    def _():
+        add_up(zb, lambda s: zqr.at[s], zothers, tot)
+
+    gl[z, quarter(yh)] = (tot[...] / ROWS).astype(BF16)
+    for d in (1, 3, 2):
+        g = gl.at[z, quarter(yh)]
+        send(g, g, as_.at[d], ar.at[yh], ydev[d])
+    for d in (1, 3, 2):
+        arrived(gl.at[z, quarter(at_y(d))], as_.at[0], ar.at[at_y(d)])
+    top = pl.ds(k * h, h)
+    low = pl.ds((1 - k) * h, h)
+    gram = gl[z, pl.ds(0, h)]
+    gr[c, top, :] = gram
 
     for n in range(2):
         send(g_col(c, n), g_col(c, n), gys.at[n], gyr.at[n], ypair)
@@ -200,9 +292,9 @@
     for b in order:
         g = gr.at[b, low]
         arrived(g, gcs.at[0], gcr.at[b])
-    square = jnp.dot(gl[0], gr[0], preferred_element_type=F32)
+    square = jnp.dot(gl[0, :h], gr[block(0)], preferred_element_type=F32)
     for s in range(1, NB):
-        square = square + jnp.dot(gl[s], gr[s], preferred_element_type=F32)
+        square = square + jnp.dot(gl[s, :h], gr[block(s)], preferred_element_type=F32)
     pf[z, top, :] = (coef_b * gram.astype(F32) + coef_c * square).astype(BF16)
     pring = (p_row, pzs, pzr, zdev, zslots)
     ring_step(*pring, 0)
@@ -211,7 +303,7 @@
     def term(s):
         arrived(pf.at[s, low], pcs.at[0], pcr.at[s])
         return lax.dot_general(
-            xx[s, pl.ds(k * m, m)], pf[s], (((1,), (1,)), ((), ())), preferred_element_type=F32
+            xx[block(s), pl.ds(k * m, m)], pf[s], (((1,), (1,)), ((), ())), preferred_element_type=F32
         )
 
     update = term(z)
@@ -229,17 +321,26 @@
         copy.wait_send()
     for i, b in enumerate(order):
 
-        @pl.when(b != z)
+        @pl.when(owner(b) != z)
         def _():
+            src = sb.at[i] if i < EARLY else qb.at[i - EARLY]
             pltpu.make_async_remote_copy(
-                src_ref=sb.at[i], dst_ref=rb.at[z], send_sem=zs.at[i], recv_sem=zr.at[z],
-                device_id=core, device_id_type=MESH,
+                src_ref=src, dst_ref=src, send_sem=zs.at[i], recv_sem=zr.at[z], device_id=core, device_id_type=MESH
+            ).wait_send()
+
+    @pl.when(mine_early)
+    def _():
+        for d in (1, 3, 2):
+            pltpu.make_async_remote_copy(
+                src_ref=eb.at[quarter(at_y(d))], dst_ref=yb.at[NB - EARLY, yh], send_sem=ys.at[NB - EARLY, d],
+                recv_sem=yr.at[NB - EARLY, yh], device_id=core, device_id_type=MESH,
             ).wait_send()
 
 
 def local(momentum):
     m, w = momentum.shape
     h = w // 2
+    q = -(-h // (16 * NY)) * 16
     dma = lambda *n: pltpu.SemaphoreType.DMA(n)
     return pl.pallas_call(
         kernel,
@@ -248,16 +349,20 @@
         out_specs=pl.BlockSpec(memory_space=pltpu.VMEM),
         scratch_shapes=[
             pltpu.VMEM((NB, 2 * m, w), BF16),
-            pltpu.VMEM((NB, h, w), BF16),
-            pltpu.VMEM((NZ, h, w), BF16),
-            pltpu.VMEM((NY, h, w), BF16),
-            pltpu.VMEM((NZ, h, w), BF16),
+            pltpu.VMEM((NB, NY * q, w), BF16),
+            pltpu.VMEM((NZ, NY * q, w), BF16),
+            pltpu.VMEM((NY * q, w), BF16),
+            pltpu.VMEM((NB - EARLY + 1, NY, q, w), BF16),
+            pltpu.VMEM((NB - EARLY, q, w), BF16),
+            pltpu.VMEM((NZ, q, w), BF16),
+            pltpu.VMEM((q, w), F32),
+            pltpu.VMEM((NZ, NY * q, w), BF16),
             pltpu.VMEM((NB, w, w), BF16),
             pltpu.VMEM((NZ, w, w), BF16),
-            pltpu.VMEM((h, 2 * m), BF16),
+            pltpu.VMEM((NY * q, 2 * m), BF16),
             pltpu.SemaphoreType.DMA,
-            dma(7), dma(8), dma(8), dma(8),
-            dma(8), dma(8), dma(4), dma(4),
+            dma(2), dma(2), dma(2, 2, 2), dma(8, 2), dma(2, 2, 2), dma(8, 2), dma(3), dma(8), dma(8), dma(8),
+            dma(8), dma(8), dma(8), dma(NB - EARLY + 1, 4), dma(NB - EARLY + 1, 4), dma(4), dma(4),
             dma(4, 2, 2), dma(8, 2), dma(2), dma(2), dma(2, 2, 2), dma(2, 2, 2), dma(8, 2), dma(8), dma(8),
             dma(4, 2, 2), dma(8, 2), dma(8), dma(8),
         ],

time: 117 us -> 104 us (0.89)
  Pallas kernels: 115 us -> 102 us
    pallas_call x1, Pallas kernels: 115 us -> 102 us  [local(): pl.pallas_call(kernel, out_shape=jax.ShapeDtypeStruct((m, w), BF16), in_s...]
where the time goes in v3:
time: 104 us
  Pallas kernels  102 us (98%)
  local copies, waits for them, and re-layouts  1.69 us (2%)
    pallas_call x1, Pallas kernels, local(): pl.pallas_call(kernel, out_shape=jax.ShapeDtypeStruct((m, w), BF16), in_s...  102 us

profile of v3, /device:TPU:1, one launch (start us, length us, event | category | flops | bytes accessed | tf_op | source)
XLA Modules:
  0.0 103.6 jit_solution(9707748598555004891)
XLA Ops:
  0.0 0.0 copy-start
  0.0 1.0 copy-done
  1.0 101.9 %newton_schulz.1 = bf16[400,352]{1,0:T(8,128)(2,1)S(1)} custom-call(bf16[400,352]{1,0:T(8,128)(2,1)S(1)} %copy-done), custom_call_target="tpu_custom_call" | custom-call | tf_op jit(solution)/shard_map/newton_schulz/pallas_call | solution.py:345
  102.9 0.7 copy.3
Async XLA Ops:
  0.0 1.0 copy-start

commit v4 on v3

v4 whole, which is shorter than its diff:
```python
import jax
import jax.numpy as jnp
from jax import lax
from jax.experimental import pallas as pl
from jax.experimental.pallas import tpu as pltpu
from jax.sharding import PartitionSpec as P

ROWS = 25600

coef_a = 3.4445
coef_b = -4.775
coef_c = 2.0315

NZ, NY, NX = 8, 4, 4
NB = 8
EARLY = 4
UP = 208
MESH = pl.DeviceIdType.MESH
F32, BF16 = jnp.float32, jnp.bfloat16


def kernel(
    x_hbm, o_ref, xx, sb, rb, eb, yb, qb, zb, tot, gl, gr, pf, lt,
    loc, xs, cs, zs, zqs, ys, es, as_, gzs, gxs, gcs, pzs, pcs,
    wr, xr, xr2, vyr, cr, zr, zqr, yr, ar, gzr, gyr, gxr, gcr, pzr, pcr,
):
    m, w = x_hbm.shape
    h = w // 2
    q = qb.shape[1]
    hp = NY * q
    cut = -(-h // 32) * 16
    mid = -(-m // 32) * 16
    up = UP
    qtr = -(-up // 32) * 16
    r, c = lax.axis_index("rows"), lax.axis_index("cols")
    z, yh, k = r // (NY * 2), lax.rem(r // 2, NY), lax.rem(r, 2)
    yl, x = c // NX, lax.rem(c, NX)

    def rid(z=z, yh=yh, k=k):
        return (z * NY + yh) * 2 + k

    def cid(yl=yl, x=x):
        return yl * NX + x

    def at_x(d):
        return lax.rem(x + d, NX)

    def at_z(d):
        return lax.rem(z + d, NZ)

    def at_y(d):
        return lax.rem(yh + d, NY)

    core = (rid(k=1 - k), c)
    ypair = (r, cid(yl=1 - yl))
    xdev = [(r, cid(x=at_x(d))) for d in range(NX)]
    zdev = [(rid(z=at_z(d)), c) for d in range(NZ)]
    ydev = [(rid(yh=at_y(d)), c) for d in range(NY)]

    def copy(src, dst, ss, rs, to):
        return pltpu.make_async_remote_copy(
            src_ref=src, dst_ref=dst, send_sem=ss, recv_sem=rs, device_id=to, device_id_type=MESH
        )

    def send(src, dst, ss, rs, to):
        copy(src, dst, ss, rs, to).start()

    def arrived(dst, rs):
        copy(dst, dst, loc, rs, core).wait_recv()

    def sent(src, ss):
        copy(src, src, ss, loc, core).wait_send()

    mine = xx.at[c, pl.ds(k * m, m)]
    own = pltpu.make_async_copy(x_hbm, mine, loc)
    own.start()
    barrier = pltpu.get_barrier_semaphore()
    partners = [core, ypair] + xdev[1:] + zdev[1:] + ydev[1:]
    for to in partners:
        pl.semaphore_signal(barrier, inc=1, device_id=to, device_id_type=MESH)
    pl.semaphore_wait(barrier, len(partners))
    own.wait()

    xslots = [cid(x=at_x(d)) for d in range(NX)]
    xslots2 = [cid(yl=1 - yl, x=at_x(d)) for d in range(NX)]
    zslots = [at_z(d) for d in range(NZ)]
    order = [xslots[0], xslots2[0]] + [xslots[d] for d in (1, 3, 2)] + [xslots2[d] for d in (1, 3, 2)]
    c2 = order[1]

    def owner(b):
        return lax.rem(b, NX) * 2 + b // NX

    def block(s):
        return s % 2 * NX + s // 2 if isinstance(s, int) else lax.rem(s, 2) * NX + s // 2

    def ring_hop(buf, ss, rs, dev, slots, hop, right, n):
        reach = len(slots) // 2 - (right == n)
        if hop > reach:
            return
        s = slots[-hop if right else hop] if hop else slots[0]
        if hop:
            arrived(buf(s, n), rs(s, n))
        if hop < reach:
            send(buf(s, n), buf(s, n), ss, rs(s, n), dev[1 if right else -1])

    def ring_step(*args):
        for right, n in ((1, 0), (0, 1), (1, 1), (0, 0)):
            ring_hop(*args, right, n)

    def half(b):
        return xx.at[b, pl.ds(k * m, m)]

    def other(b):
        return xx.at[b, pl.ds((1 - k) * m, m)]

    def x_half(b, n):
        return xx.at[b, pl.ds(k * m + n * mid, m - mid if n else mid)]

    def x_quarter(b, n):
        return xx.at[b, pl.ds(k * m + n * qtr, up - qtr if n else qtr)]

    def x_rest(i):
        return xx.at[order[i], pl.ds(k * m + up, m - up)]

    def over(i):
        send(x_rest(i), x_rest(i), xs, vyr.at[lax.rem(order[i], NX)], ypair)

    def back(i):
        arrived(x_rest(i), vyr.at[lax.rem(order[i], NX)])

    def hand(i):
        send(half(order[i]), half(order[i]), cs, cr.at[order[i]], core)

    def quarter(p):
        return pl.ds(pl.multiple_of(p * q, q), q)

    def to_owner(i, src, dst, ss, rs):
        to = owner(order[i])

        @pl.when(to != z)
        def _():
            send(src, dst.at[z], ss, rs, (rid(z=to), c))

        @pl.when(to == z)
        def _():
            dst[z] = src[...]

    def add_up(buf, out):
        value = buf[0].astype(F32)
        for s in range(1, buf.shape[0]):
            value = value + buf[s].astype(F32)
        out[...] = value.astype(out.dtype)

    def partial(i):
        b = order[i]
        if i:
            arrived(other(b), cr.at[b])
        sb[i] = jnp.dot(lt[...], xx[b], preferred_element_type=F32).astype(BF16)
        if i < EARLY:
            to_owner(i, sb.at[i], rb, zs, zr)
        else:
            j = i - EARLY
            yb[j, yh] = sb[i, quarter(yh)]
            for d in (1, 3, 2):
                send(sb.at[i, quarter(at_y(d))], yb.at[j, yh], ys, yr.at[j], ydev[d])

    def late(i):
        j = i - EARLY
        arrived(yb.at[j, pl.ds(0, NY - 1)], yr.at[j])
        add_up(yb.at[j], qb.at[j])
        to_owner(i, qb.at[j], zb, zqs, zqr)

    rring = (x_half, xs, lambda b, n: xr.at[lax.rem(b, NX), n], xdev, xslots)
    rring2 = (x_quarter, xs, lambda b, n: xr2.at[lax.rem(b, NX), n], xdev, xslots2)
    send(half(c), half(c), xs, wr, ypair)
    ring_step(*rring, 0)
    hand(0)
    pick = (
        lax.broadcasted_iota(jnp.int32, (hp, w), 1) == lax.broadcasted_iota(jnp.int32, (hp, w), 0) + k * h
    ).astype(BF16)
    arrived(other(c), cr.at[c])
    lt[...] = lax.dot_general(
        pick, xx[c], (((1,), (1,)), ((), ())), preferred_element_type=F32
    ).astype(BF16)
    partial(0)
    arrived(half(c2), wr)
    hand(1)
    ring_step(*rring, 1)
    over(2)
    over(3)
    hand(2)
    hand(3)
    ring_step(*rring2, 0)
    partial(1)
    partial(2)
    partial(3)
    ring_step(*rring, 2)
    over(4)
    hand(4)
    ring_step(*rring2, 1)
    for i in (5, 6):
        back(i)
        hand(i)
    partial(4)
    partial(5)
    partial(6)
    ring_step(*rring2, 2)
    back(7)
    hand(7)
    partial(7)
    for i in range(EARLY, NB):
        late(i)

    mine_early = owner(order[0]) == z
    for i in range(1, EARLY):
        mine_early = jnp.logical_or(mine_early, owner(order[i]) == z)

    @pl.when(mine_early)
    def _():
        arrived(rb.at[pl.ds(0, NZ - 1)], zr)
        add_up(rb, eb)
        yb[NB - EARLY, yh] = eb[quarter(yh)]
        for d in (1, 3, 2):
            send(eb.at[quarter(at_y(d))], yb.at[NB - EARLY, yh], es, yr.at[NB - EARLY], ydev[d])
        arrived(yb.at[NB - EARLY, pl.ds(0, NY - 1)], yr.at[NB - EARLY])
        add_up(yb.at[NB - EARLY], tot)

    @pl.when(jnp.logical_not(mine_early))
    def _():
        arrived(zb.at[pl.ds(0, NZ - 1)], zqr)
        add_up(zb, tot)

    gl[z, quarter(yh)] = (tot[...] / ROWS).astype(BF16)
    for d in (1, 3, 2):
        g = gl.at[z, quarter(yh)]
        send(g, g, as_, ar, ydev[d])
    arrived(gl.at[z, pl.ds(0, hp - q)], ar)
    top = pl.ds(k * h, h)
    low = pl.ds((1 - k) * h, h)
    gram = gl[z, pl.ds(0, h)]
    gr[c, top, :] = gram

    def part(base, n):
        return pl.ds(base + n * cut, h - cut if n else cut)

    def g_row(s, n):
        return gl.at[s, part(0, n)]

    def g_col(b, n):
        return gr.at[b, part(k * h, n)]

    def p_row(s, n):
        return pf.at[s, part(k * h, n)]

    zring = (g_row, gzs, lambda s, n: gzr.at[s, n], zdev, zslots)
    xring = (g_col, gxs, lambda s, n: gxr.at[s, n], xdev, xslots)
    xring2 = (g_col, gxs, lambda s, n: gxr.at[s, n], xdev, xslots2)

    def hand_on(slots):
        for b in slots:
            send(gr.at[b, top], gr.at[b, top], gcs, gcr, core)

    send(gr.at[c, top], gr.at[c, top], gxs, gyr, ypair)
    ring_step(*xring, 0)
    ring_step(*zring, 0)
    hand_on([c])
    arrived(gr.at[c2, top], gyr)
    ring_step(*xring2, 0)
    hand_on([c2])
    ring_step(*xring, 1)
    ring_step(*zring, 1)
    hand_on([xslots[1], xslots[3]])
    ring_step(*xring, 2)
    ring_step(*zring, 2)
    hand_on([xslots[2]])
    ring_step(*xring2, 1)
    hand_on([xslots2[1], xslots2[3]])
    ring_step(*zring, 3)
    ring_step(*xring2, 2)
    hand_on([xslots2[2]])
    ring_step(*zring, 4)
    arrived(gr.at[:, pl.ds(0, h)], gcr)
    square = jnp.dot(gl[0, :h], gr[block(0)], preferred_element_type=F32)
    for s in range(1, NB):
        square = square + jnp.dot(gl[s, :h], gr[block(s)], preferred_element_type=F32)
    pf[z, top, :] = (coef_b * gram.astype(F32) + coef_c * square).astype(BF16)
    pring = (p_row, pzs, lambda s, n: pzr.at[s, n], zdev, zslots)

    def hand_over(slots):
        for s in slots:
            send(pf.at[s, top], pf.at[s, top], pcs, pcr.at[s], core)

    def term(s):
        arrived(pf.at[s, low], pcr.at[s])
        return lax.dot_general(
            xx[block(s), pl.ds(k * m, m)], pf[s], (((1,), (1,)), ((), ())), preferred_element_type=F32
        )

    ring_step(*pring, 0)
    hand_over([z])
    update = None
    held = [z]
    for step in range(1, 5):
        ring_step(*pring, step)
        got = [zslots[-step], zslots[step]] if step < 4 else [zslots[4]]
        hand_over(got)
        for s in held:
            update = term(s) if update is None else update + term(s)
        held = got
    for s in held:
        update = update + term(s)
    o_ref[...] = (coef_a * xx[c, pl.ds(k * m, m)].astype(F32) + update).astype(BF16)

    sent(xx.at[pl.ds(0, NB - 1), pl.ds(0, m)], xs)
    sent(xx.at[:, pl.ds(0, m)], cs)

    @pl.when(mine_early)
    def _():
        sent(sb.at[pl.ds(0, EARLY - 1)], zs)
        sent(qb, zqs)
        sent(eb.at[pl.ds(0, hp - q)], es)

    @pl.when(jnp.logical_not(mine_early))
    def _():
        sent(sb.at[pl.ds(0, EARLY)], zs)
        sent(qb.at[pl.ds(0, NB - EARLY - 1)], zqs)

    sent(yb.at[pl.ds(0, NB - EARLY), pl.ds(0, NY - 1)], ys)
    sent(gl.at[z, pl.ds(0, hp - q)], as_)
    sent(gl.at[pl.ds(0, NZ - 1), pl.ds(0, h)], gzs)
    sent(gr.at[pl.ds(0, NB - 1), pl.ds(0, h)], gxs)
    sent(gr.at[:, pl.ds(0, h)], gcs)
    sent(pf.at[pl.ds(0, NZ - 1), pl.ds(0, h)], pzs)
    sent(pf.at[:, pl.ds(0, h)], pcs)


def local(momentum):
    m, w = momentum.shape
    h = w // 2
    q = -(-h // (16 * NY)) * 16
    dma = lambda *n: pltpu.SemaphoreType.DMA(n)
    one = pltpu.SemaphoreType.DMA
    return pl.pallas_call(
        kernel,
        out_shape=jax.ShapeDtypeStruct((m, w), BF16),
        in_specs=[pl.BlockSpec(memory_space=pl.ANY)],
        out_specs=pl.BlockSpec(memory_space=pltpu.VMEM),
        scratch_shapes=[
            pltpu.VMEM((NB, 2 * m, w), BF16),
            pltpu.VMEM((NB, NY * q, w), BF16),
            pltpu.VMEM((NZ, NY * q, w), BF16),
            pltpu.VMEM((NY * q, w), BF16),
            pltpu.VMEM((NB - EARLY + 1, NY, q, w), BF16),
            pltpu.VMEM((NB - EARLY, q, w), BF16),
            pltpu.VMEM((NZ, q, w), BF16),
            pltpu.VMEM((q, w), F32),
            pltpu.VMEM((NZ, NY * q, w), BF16),
            pltpu.VMEM((NB, w, w), BF16),
            pltpu.VMEM((NZ, w, w), BF16),
            pltpu.VMEM((NY * q, 2 * m), BF16),
            one, one, one, one, one, one, one, one, one, one, one, one, one,
            one, dma(NX, 2), dma(NX, 2), dma(NX), dma(NB), one, one, dma(NB - EARLY + 1), one,
            dma(NZ, 2), one, dma(NB, 2), one, dma(NZ, 2), dma(NZ),
        ],
        compiler_params=pltpu.CompilerParams(
            collective_id=0, has_side_effects=True, vmem_limit_bytes=48 << 20
        ),
        name="newton_schulz",
    )(momentum)


def solution(mesh):
    return jax.shard_map(
        local,
        mesh=mesh,
        in_specs=(P("rows", "cols"),),
        out_specs=P("rows", "cols"),
        check_vma=False,
    )
```

time: 104 us -> 97.9 us (0.941)
  Pallas kernels: 102 us -> 96.1 us
    pallas_call x1, Pallas kernels: 102 us -> 96.1 us  [local(): pl.pallas_call(kernel, out_shape=jax.ShapeDtypeStruct((m, w), BF16), in_s...]
where the time goes in v4:
time: 97.9 us; the launch traced here: 97.8 us
  Pallas kernels  96.1 us (98%)
  local copies, waits for them, and re-layouts  1.69 us (2%)
    pallas_call x1, Pallas kernels, local(): pl.pallas_call(kernel, out_shape=jax.ShapeDtypeStruct((m, w), BF16), in_s...  96.1 us

profile of v4, /device:TPU:1, one launch (start us, length us, event | category | flops | bytes accessed | tf_op | source)
XLA Modules:
  0.0 97.8 jit_solution(6212266685518068830)
XLA Ops:
  0.0 0.0 copy-start
  0.0 1.0 copy-done
  1.0 96.1 %newton_schulz.1 = bf16[400,352]{1,0:T(8,128)(2,1)S(1)} custom-call(bf16[400,352]{1,0:T(8,128)(2,1)S(1)} %copy-done), custom_call_target="tpu_custom_call" | custom-call | tf_op jit(solution)/shard_map/newton_schulz/pallas_call | solution.py:343
  97.0 0.7 copy.3
Async XLA Ops:
  0.0 1.0 copy-start

commit v5 on v4

--- a/solution.py
+++ b/solution.py
@@ -14,7 +14,7 @@
 NZ, NY, NX = 8, 4, 4
 NB = 8
 EARLY = 4
-UP = 208
+UP = 256
 MESH = pl.DeviceIdType.MESH
 F32, BF16 = jnp.float32, jnp.bfloat16
 
@@ -75,7 +75,7 @@
     own = pltpu.make_async_copy(x_hbm, mine, loc)
     own.start()
     barrier = pltpu.get_barrier_semaphore()
-    partners = [core, ypair] + xdev[1:] + zdev[1:] + ydev[1:]
+    partners = [core, ypair] + xdev[1:] + [(r, cid(yl=1 - yl, x=at_x(d))) for d in (1, 2, 3)] + zdev[1:] + ydev[1:]
     for to in partners:
         pl.semaphore_signal(barrier, inc=1, device_id=to, device_id_type=MESH)
     pl.semaphore_wait(barrier, len(partners))
@@ -183,14 +183,14 @@
         pick, xx[c], (((1,), (1,)), ((), ())), preferred_element_type=F32
     ).astype(BF16)
     partial(0)
-    arrived(half(c2), wr)
-    hand(1)
     ring_step(*rring, 1)
     over(2)
     over(3)
     hand(2)
     hand(3)
+    arrived(half(c2), wr)
     ring_step(*rring2, 0)
+    hand(1)
     partial(1)
     partial(2)
     partial(3)
@@ -208,9 +208,6 @@
     back(7)
     hand(7)
     partial(7)
-    for i in range(EARLY, NB):
-        late(i)
-
     mine_early = owner(order[0]) == z
     for i in range(1, EARLY):
         mine_early = jnp.logical_or(mine_early, owner(order[i]) == z)
@@ -222,6 +219,12 @@
         yb[NB - EARLY, yh] = eb[quarter(yh)]
         for d in (1, 3, 2):
             send(eb.at[quarter(at_y(d))], yb.at[NB - EARLY, yh], es, yr.at[NB - EARLY], ydev[d])
+
+    for i in range(EARLY, NB):
+        late(i)
+
+    @pl.when(mine_early)
+    def _():
         arrived(yb.at[NB - EARLY, pl.ds(0, NY - 1)], yr.at[NB - EARLY])
         add_up(yb.at[NB - EARLY], tot)
 
@@ -260,24 +263,19 @@
         for b in slots:
             send(gr.at[b, top], gr.at[b, top], gcs, gcr, core)
 
-    send(gr.at[c, top], gr.at[c, top], gxs, gyr, ypair)
-    ring_step(*xring, 0)
+    for to in [ypair] + [xdev[d] for d in (1, 3, 2)] + [(r, xslots2[d]) for d in (1, 3, 2)]:
+        send(gr.at[c, top], gr.at[c, top], gxs, gxr.at[c, 0], to)
     ring_step(*zring, 0)
     hand_on([c])
-    arrived(gr.at[c2, top], gyr)
-    ring_step(*xring2, 0)
-    hand_on([c2])
-    ring_step(*xring, 1)
     ring_step(*zring, 1)
-    hand_on([xslots[1], xslots[3]])
-    ring_step(*xring, 2)
     ring_step(*zring, 2)
-    hand_on([xslots[2]])
-    ring_step(*xring2, 1)
-    hand_on([xslots2[1], xslots2[3]])
+    for b in order[1:5]:
+        arrived(gr.at[b, top], gxr.at[b, 0])
+        hand_on([b])
     ring_step(*zring, 3)
-    ring_step(*xring2, 2)
-    hand_on([xslots2[2]])
+    for b in order[5:]:
+        arrived(gr.at[b, top], gxr.at[b, 0])
+        hand_on([b])
     ring_step(*zring, 4)
     arrived(gr.at[:, pl.ds(0, h)], gcr)
     square = jnp.dot(gl[0, :h], gr[block(0)], preferred_element_type=F32)

time: 97.9 us -> 96.2 us (0.983)
  Pallas kernels: 96.1 us -> 94.3 us
    pallas_call x1, Pallas kernels: 96.1 us -> 94.3 us  [local(): pl.pallas_call(kernel, out_shape=jax.ShapeDtypeStruct((m, w), BF16), in_s...]
where the time goes in v5:
time: 96.2 us; the launch traced here: 96 us
  Pallas kernels  94.3 us (98%)
  local copies, waits for them, and re-layouts  1.69 us (2%)
    pallas_call x1, Pallas kernels, local(): pl.pallas_call(kernel, out_shape=jax.ShapeDtypeStruct((m, w), BF16), in_s...  94.3 us

profile of v5, /device:TPU:1, one launch (start us, length us, event | category | flops | bytes accessed | tf_op | source)
XLA Modules:
  0.0 96.0 jit_solution(1680120069586278471)
XLA Ops:
  0.0 0.0 copy-start
  0.0 1.0 %copy-done = bf16[400,352]{1,0:T(8,128)(2,1)S(1)} copy-done((bf16[400,352]{1,0:T(8,128)(2,1)S(1)}, bf16[400,352]{1,0:T(8,128)(2,1)}, u32[]{:S(2)}) %copy-start) | copy-done | bytes 281624
  1.0 94.3 %newton_schulz.1 = bf16[400,352]{1,0:T(8,128)(2,1)S(1)} custom-call(bf16[400,352]{1,0:T(8,128)(2,1)S(1)} %copy-done), custom_call_target="tpu_custom_call" | custom-call | tf_op jit(solution)/shard_map/newton_schulz/pallas_call | solution.py:341
  95.2 0.7 copy.3
Async XLA Ops:
  0.0 1.0 %copy-start = (bf16[400,352]{1,0:T(8,128)(2,1)S(1)}, bf16[400,352]{1,0:T(8,128)(2,1)}, u32[]{:S(2)}) copy-start(bf16[400,352]{1,0:T(8,128)(2,1)} %x_hbm.1) | copy-start | bytes 844804

commit v6 on v5

--- a/solution.py
+++ b/solution.py
@@ -22,12 +22,13 @@
 def kernel(
     x_hbm, o_ref, xx, sb, rb, eb, yb, qb, zb, tot, gl, gr, pf, lt,
     loc, xs, cs, zs, zqs, ys, es, as_, gzs, gxs, gcs, pzs, pcs,
-    wr, xr, xr2, vyr, cr, zr, zqr, yr, ar, gzr, gyr, gxr, gcr, pzr, pcr,
+    wr, xr, xr2, vyr, cr, zr, zqr, yr, ar, gzr, gxr, gcr, pzr, pcr,
 ):
     m, w = x_hbm.shape
     h = w // 2
     q = qb.shape[1]
     hp = NY * q
+    ql = h - (NY - 1) * q
     cut = -(-h // 32) * 16
     mid = -(-m // 32) * 16
     up = UP
@@ -133,6 +134,22 @@
 
     def quarter(p):
         return pl.ds(pl.multiple_of(p * q, q), q)
+
+    def with_quarter(p, do):
+        @pl.when(p < NY - 1)
+        def _():
+            do(quarter(p), q)
+
+        @pl.when(p == NY - 1)
+        def _():
+            do(pl.ds((NY - 1) * q, ql), ql)
+
+    def spread(src, dst, ss, rs):
+        for d in (1, 3, 2):
+            with_quarter(at_y(d), lambda rows, n: send(src.at[rows], dst.at[yh, pl.ds(0, n)], ss, rs, ydev[d]))
+
+    def quarters_in(buf, rs):
+        with_quarter(yh, lambda rows, n: arrived(buf.at[pl.ds(0, NY - 1), pl.ds(0, n)], rs))
 
     def to_owner(i, src, dst, ss, rs):
         to = owner(order[i])
@@ -161,12 +178,11 @@
         else:
             j = i - EARLY
             yb[j, yh] = sb[i, quarter(yh)]
-            for d in (1, 3, 2):
-                send(sb.at[i, quarter(at_y(d))], yb.at[j, yh], ys, yr.at[j], ydev[d])
+            spread(sb.at[i], yb.at[j], ys, yr.at[j])
 
     def late(i):
         j = i - EARLY
-        arrived(yb.at[j, pl.ds(0, NY - 1)], yr.at[j])
+        quarters_in(yb.at[j], yr.at[j])
         add_up(yb.at[j], qb.at[j])
         to_owner(i, qb.at[j], zb, zqs, zqr)
 
@@ -217,15 +233,14 @@
         arrived(rb.at[pl.ds(0, NZ - 1)], zr)
         add_up(rb, eb)
         yb[NB - EARLY, yh] = eb[quarter(yh)]
-        for d in (1, 3, 2):
-            send(eb.at[quarter(at_y(d))], yb.at[NB - EARLY, yh], es, yr.at[NB - EARLY], ydev[d])
+        spread(eb, yb.at[NB - EARLY], es, yr.at[NB - EARLY])
 
     for i in range(EARLY, NB):
         late(i)
 
     @pl.when(mine_early)
     def _():
-        arrived(yb.at[NB - EARLY, pl.ds(0, NY - 1)], yr.at[NB - EARLY])
+        quarters_in(yb.at[NB - EARLY], yr.at[NB - EARLY])
         add_up(yb.at[NB - EARLY], tot)
 
     @pl.when(jnp.logical_not(mine_early))
@@ -233,55 +248,80 @@
         arrived(zb.at[pl.ds(0, NZ - 1)], zqr)
         add_up(zb, tot)
 
-    gl[z, quarter(yh)] = (tot[...] / ROWS).astype(BF16)
-    for d in (1, 3, 2):
-        g = gl.at[z, quarter(yh)]
-        send(g, g, as_, ar, ydev[d])
-    arrived(gl.at[z, pl.ds(0, hp - q)], ar)
     top = pl.ds(k * h, h)
     low = pl.ds((1 - k) * h, h)
-    gram = gl[z, pl.ds(0, h)]
-    gr[c, top, :] = gram
-
-    def part(base, n):
-        return pl.ds(base + n * cut, h - cut if n else cut)
-
-    def g_row(s, n):
-        return gl.at[s, part(0, n)]
-
-    def g_col(b, n):
-        return gr.at[b, part(k * h, n)]
-
-    def p_row(s, n):
-        return pf.at[s, part(k * h, n)]
-
-    zring = (g_row, gzs, lambda s, n: gzr.at[s, n], zdev, zslots)
-    xring = (g_col, gxs, lambda s, n: gxr.at[s, n], xdev, xslots)
-    xring2 = (g_col, gxs, lambda s, n: gxr.at[s, n], xdev, xslots2)
+    columns = [ypair] + [xdev[d] for d in (1, 3, 2)] + [(r, xslots2[d]) for d in (1, 3, 2)]
+
+    def over_z(s, rows, j, hop, right):
+        if hop < NZ // 2 - (right == j % 2):
+            g = gl.at[s, rows]
+            send(g, g, gzs, gzr.at[s, j], zdev[1 if right else -1])
+
+    def set_off(j):
+        def go(rows, n):
+            g = gl.at[z, rows]
+            if j == 0:
+                gl[z, rows] = (tot[pl.ds(0, n)] / ROWS).astype(BF16)
+                for d in (1, 3, 2):
+                    send(g, g, as_, ar.at[NY - d], ydev[d])
+            else:
+                arrived(g, ar.at[j])
+            for right in (1, 0):
+                over_z(z, rows, j, 0, right)
+            for to in columns:
+                send(g, gr.at[c, pl.ds(pl.multiple_of(k * h + rows.start, 16), n)], gxs, gxr.at[c], to)
+
+        with_quarter(at_y(j), go)
+
+    def hops(step, js):
+        for j in js:
+            for right in (1, 0):
+                if step <= NZ // 2 - (right == j % 2):
+                    s = zslots[-step if right else step]
+
+                    def go(rows, n):
+                        arrived(gl.at[s, rows], gzr.at[s, j])
+                        over_z(s, rows, j, step, right)
+
+                    with_quarter(at_y(j), go)
 
     def hand_on(slots):
         for b in slots:
             send(gr.at[b, top], gr.at[b, top], gcs, gcr, core)
 
-    for to in [ypair] + [xdev[d] for d in (1, 3, 2)] + [(r, xslots2[d]) for d in (1, 3, 2)]:
-        send(gr.at[c, top], gr.at[c, top], gxs, gxr.at[c, 0], to)
-    ring_step(*zring, 0)
+    def columns_in(slots):
+        for b in slots:
+            arrived(gr.at[b, top], gxr.at[b])
+            hand_on([b])
+
+    set_off(0)
+    set_off(1)
+    set_off(3)
+    hops(1, (0,))
+    set_off(2)
+    gram = gl[z]
+    gr[c, top, :] = gram
     hand_on([c])
-    ring_step(*zring, 1)
-    ring_step(*zring, 2)
-    for b in order[1:5]:
-        arrived(gr.at[b, top], gxr.at[b, 0])
-        hand_on([b])
-    ring_step(*zring, 3)
-    for b in order[5:]:
-        arrived(gr.at[b, top], gxr.at[b, 0])
-        hand_on([b])
-    ring_step(*zring, 4)
+    hops(1, (1, 3))
+    hops(2, (0,))
+    hops(1, (2,))
+    hops(2, (1, 3))
+    hops(3, (0,))
+    hops(2, (2,))
+    columns_in(order[1:4])
+    hops(3, (1, 3))
+    hops(4, (0,))
+    hops(3, (2,))
+    columns_in(order[4:])
+    hops(4, (1, 3, 2))
     arrived(gr.at[:, pl.ds(0, h)], gcr)
-    square = jnp.dot(gl[0, :h], gr[block(0)], preferred_element_type=F32)
+    square = jnp.dot(gl[0], gr[block(0)], preferred_element_type=F32)
     for s in range(1, NB):
-        square = square + jnp.dot(gl[s, :h], gr[block(s)], preferred_element_type=F32)
+        square = square + jnp.dot(gl[s], gr[block(s)], preferred_element_type=F32)
     pf[z, top, :] = (coef_b * gram.astype(F32) + coef_c * square).astype(BF16)
+    def p_row(s, n):
+        return pf.at[s, pl.ds(k * h + n * cut, h - cut if n else cut)]
+
     pring = (p_row, pzs, lambda s, n: pzr.at[s, n], zdev, zslots)
 
     def hand_over(slots):
@@ -316,16 +356,16 @@
     def _():
         sent(sb.at[pl.ds(0, EARLY - 1)], zs)
         sent(qb, zqs)
-        sent(eb.at[pl.ds(0, hp - q)], es)
+        with_quarter(yh, lambda rows, n: sent(eb.at[pl.ds(0, h - n)], es))
 
     @pl.when(jnp.logical_not(mine_early))
     def _():
         sent(sb.at[pl.ds(0, EARLY)], zs)
         sent(qb.at[pl.ds(0, NB - EARLY - 1)], zqs)
 
-    sent(yb.at[pl.ds(0, NB - EARLY), pl.ds(0, NY - 1)], ys)
-    sent(gl.at[z, pl.ds(0, hp - q)], as_)
-    sent(gl.at[pl.ds(0, NZ - 1), pl.ds(0, h)], gzs)
+    with_quarter(yh, lambda rows, n: sent(sb.at[pl.ds(0, NB - EARLY), pl.ds(0, h - n)], ys))
+    with_quarter(yh, lambda rows, n: sent(gl.at[pl.ds(0, NY - 1), pl.ds(0, n)], as_))
+    sent(gl.at[pl.ds(0, NZ - 1)], gzs)
     sent(gr.at[pl.ds(0, NB - 1), pl.ds(0, h)], gxs)
     sent(gr.at[:, pl.ds(0, h)], gcs)
     sent(pf.at[pl.ds(0, NZ - 1), pl.ds(0, h)], pzs)
@@ -352,13 +392,13 @@
             pltpu.VMEM((NB - EARLY, q, w), BF16),
             pltpu.VMEM((NZ, q, w), BF16),
             pltpu.VMEM((q, w), F32),
-            pltpu.VMEM((NZ, NY * q, w), BF16),
+            pltpu.VMEM((NZ, h, w), BF16),
             pltpu.VMEM((NB, w, w), BF16),
             pltpu.VMEM((NZ, w, w), BF16),
             pltpu.VMEM((NY * q, 2 * m), BF16),
             one, one, one, one, one, one, one, one, one, one, one, one, one,
-            one, dma(NX, 2), dma(NX, 2), dma(NX), dma(NB), one, one, dma(NB - EARLY + 1), one,
-            dma(NZ, 2), one, dma(NB, 2), one, dma(NZ, 2), dma(NZ),
+            one, dma(NX, 2), dma(NX, 2), dma(NX), dma(NB), one, one, dma(NB - EARLY + 1), dma(NY),
+            dma(NZ, NY), dma(NB), one, dma(NZ, 2), dma(NZ),
         ],
         compiler_params=pltpu.CompilerParams(
             collective_id=0, has_side_effects=True, vmem_limit_bytes=48 << 20

time: 96.2 us -> 94.4 us (0.981)
  Pallas kernels: 94.3 us -> 92.5 us
    pallas_call x1, Pallas kernels: 94.3 us -> 92.5 us  [local(): pl.pallas_call(kernel, out_shape=jax.ShapeDtypeStruct((m, w), BF16), in_s...]
where the time goes in v6:
time: 94.4 us; the launch traced here: 94.2 us
  Pallas kernels  92.5 us (98%)
  local copies, waits for them, and re-layouts  1.69 us (2%)
    pallas_call x1, Pallas kernels, local(): pl.pallas_call(kernel, out_shape=jax.ShapeDtypeStruct((m, w), BF16), in_s...  92.5 us

profile of v6, /device:TPU:1, one launch (start us, length us, event | category | flops | bytes accessed | tf_op | source)
XLA Modules:
  0.0 94.2 jit_solution(5230802604732766362)
XLA Ops:
  0.0 0.0 copy-start
  0.0 1.0 %copy-done = bf16[400,352]{1,0:T(8,128)(2,1)S(1)} copy-done((bf16[400,352]{1,0:T(8,128)(2,1)S(1)}, bf16[400,352]{1,0:T(8,128)(2,1)}, u32[]{:S(2)}) %copy-start) | copy-done | bytes 281624
  1.0 92.5 %newton_schulz.1 = bf16[400,352]{1,0:T(8,128)(2,1)S(1)} custom-call(bf16[400,352]{1,0:T(8,128)(2,1)S(1)} %copy-done), custom_call_target="tpu_custom_call" | custom-call | tf_op jit(solution)/shard_map/newton_schulz/pallas_call | solution.py:381
  93.5 0.7 copy.3
Async XLA Ops:
  0.0 1.0 %copy-start = (bf16[400,352]{1,0:T(8,128)(2,1)S(1)}, bf16[400,352]{1,0:T(8,128)(2,1)}, u32[]{:S(2)}) copy-start(bf16[400,352]{1,0:T(8,128)(2,1)} %x_hbm.1) | copy-start | bytes 844804

commit v7 on v6

--- a/solution.py
+++ b/solution.py
@@ -15,6 +15,7 @@
 NB = 8
 EARLY = 4
 UP = 256
+POS = 7
 MESH = pl.DeviceIdType.MESH
 F32, BF16 = jnp.float32, jnp.bfloat16
 
@@ -207,9 +208,9 @@
     arrived(half(c2), wr)
     ring_step(*rring2, 0)
     hand(1)
-    partial(1)
     partial(2)
     partial(3)
+    partial(1)
     ring_step(*rring, 2)
     over(4)
     hand(4)
@@ -228,15 +229,20 @@
     for i in range(1, EARLY):
         mine_early = jnp.logical_or(mine_early, owner(order[i]) == z)
 
-    @pl.when(mine_early)
-    def _():
-        arrived(rb.at[pl.ds(0, NZ - 1)], zr)
-        add_up(rb, eb)
-        yb[NB - EARLY, yh] = eb[quarter(yh)]
-        spread(eb, yb.at[NB - EARLY], es, yr.at[NB - EARLY])
+    def start_early():
+        @pl.when(mine_early)
+        def _():
+            arrived(rb.at[pl.ds(0, NZ - 1)], zr)
+            add_up(rb, eb)
+            yb[NB - EARLY, yh] = eb[quarter(yh)]
+            spread(eb, yb.at[NB - EARLY], es, yr.at[NB - EARLY])
 
     for i in range(EARLY, NB):
+        if i == POS:
+            start_early()
         late(i)
+    if POS == NB:
+        start_early()
 
     @pl.when(mine_early)
     def _():
@@ -310,14 +316,17 @@
     hops(2, (2,))
     columns_in(order[1:4])
     hops(3, (1, 3))
-    hops(4, (0,))
     hops(3, (2,))
     columns_in(order[4:])
-    hops(4, (1, 3, 2))
+    def square_term(s):
+        return jnp.dot(gl[s], gr[block(s)], preferred_element_type=F32)
+
     arrived(gr.at[:, pl.ds(0, h)], gcr)
-    square = jnp.dot(gl[0], gr[block(0)], preferred_element_type=F32)
-    for s in range(1, NB):
-        square = square + jnp.dot(gl[s], gr[block(s)], preferred_element_type=F32)
+    square = square_term(z)
+    for d in (1, 7, 2, 6, 3, 5):
+        square = square + square_term(zslots[d])
+    hops(4, (0, 1, 3, 2))
+    square = square + square_term(zslots[4])
     pf[z, top, :] = (coef_b * gram.astype(F32) + coef_c * square).astype(BF16)
     def p_row(s, n):
         return pf.at[s, pl.ds(k * h + n * cut, h - cut if n else cut)]

time: 94.4 us -> 92.9 us (0.984)
  Pallas kernels: 92.5 us -> 91 us
    pallas_call x1, Pallas kernels: 92.5 us -> 91 us  [local(): pl.pallas_call(kernel, out_shape=jax.ShapeDtypeStruct((m, w), BF16), in_s...]
where the time goes in v7:
time: 92.9 us; the launch traced here: 92.7 us
  Pallas kernels  91 us (98%)
  local copies, waits for them, and re-layouts  1.69 us (2%)
    pallas_call x1, Pallas kernels, local(): pl.pallas_call(kernel, out_shape=jax.ShapeDtypeStruct((m, w), BF16), in_s...  91 us

profile of v7, /device:TPU:1, one launch (start us, length us, event | category | flops | bytes accessed | tf_op | source)
XLA Modules:
  0.0 92.7 jit_solution(9019094937940893012)
XLA Ops:
  0.0 0.0 copy-start
  0.0 1.0 %copy-done = bf16[400,352]{1,0:T(8,128)(2,1)S(1)} copy-done((bf16[400,352]{1,0:T(8,128)(2,1)S(1)}, bf16[400,352]{1,0:T(8,128)(2,1)}, u32[]{:S(2)}) %copy-start) | copy-done | bytes 281624
  1.0 91.0 %newton_schulz.1 = bf16[400,352]{1,0:T(8,128)(2,1)S(1)} custom-call(bf16[400,352]{1,0:T(8,128)(2,1)S(1)} %copy-done), custom_call_target="tpu_custom_call" | custom-call | tf_op jit(solution)/shard_map/newton_schulz/pallas_call | solution.py:390
  92.0 0.7 copy.3
Async XLA Ops:
  0.0 1.0 %copy-start = (bf16[400,352]{1,0:T(8,128)(2,1)S(1)}, bf16[400,352]{1,0:T(8,128)(2,1)}, u32[]{:S(2)}) copy-start(bf16[400,352]{1,0:T(8,128)(2,1)} %x_hbm.1) | copy-start | bytes 844804

commit v8 on v7

--- a/solution.py
+++ b/solution.py
@@ -15,7 +15,7 @@
 NB = 8
 EARLY = 4
 UP = 256
-POS = 7
+START = 7
 MESH = pl.DeviceIdType.MESH
 F32, BF16 = jnp.float32, jnp.bfloat16
 
@@ -96,7 +96,7 @@
         return s % 2 * NX + s // 2 if isinstance(s, int) else lax.rem(s, 2) * NX + s // 2
 
     def ring_hop(buf, ss, rs, dev, slots, hop, right, n):
-        reach = len(slots) // 2 - (right == n)
+        reach = len(slots) // 2 - (right == n % 2)
         if hop > reach:
             return
         s = slots[-hop if right else hop] if hop else slots[0]
@@ -238,10 +238,10 @@
             spread(eb, yb.at[NB - EARLY], es, yr.at[NB - EARLY])
 
     for i in range(EARLY, NB):
-        if i == POS:
+        if i == START:
             start_early()
         late(i)
-    if POS == NB:
+    if START == NB:
         start_early()
 
     @pl.when(mine_early)
@@ -329,7 +329,11 @@
     square = square + square_term(zslots[4])
     pf[z, top, :] = (coef_b * gram.astype(F32) + coef_c * square).astype(BF16)
     def p_row(s, n):
-        return pf.at[s, pl.ds(k * h + n * cut, h - cut if n else cut)]
+        return pf.at[s, pl.ds(k * h + n * q, min(q, h - n * q))]
+
+    def ring_step4(*args):
+        for right, n in ((1, 0), (0, 1), (1, 2), (0, 3), (1, 1), (0, 0), (1, 3), (0, 2)):
+            ring_hop(*args, right, n)
 
     pring = (p_row, pzs, lambda s, n: pzr.at[s, n], zdev, zslots)
 
@@ -343,12 +347,12 @@
             xx[block(s), pl.ds(k * m, m)], pf[s], (((1,), (1,)), ((), ())), preferred_element_type=F32
         )
 
-    ring_step(*pring, 0)
+    ring_step4(*pring, 0)
     hand_over([z])
     update = None
     held = [z]
     for step in range(1, 5):
-        ring_step(*pring, step)
+        ring_step4(*pring, step)
         got = [zslots[-step], zslots[step]] if step < 4 else [zslots[4]]
         hand_over(got)
         for s in held:
@@ -407,7 +411,7 @@
             pltpu.VMEM((NY * q, 2 * m), BF16),
             one, one, one, one, one, one, one, one, one, one, one, one, one,
             one, dma(NX, 2), dma(NX, 2), dma(NX), dma(NB), one, one, dma(NB - EARLY + 1), dma(NY),
-            dma(NZ, NY), dma(NB), one, dma(NZ, 2), dma(NZ),
+            dma(NZ, NY), dma(NB), one, dma(NZ, NY), dma(NZ),
         ],
         compiler_params=pltpu.CompilerParams(
             collective_id=0, has_side_effects=True, vmem_limit_bytes=48 << 20

time: 92.9 us -> 92.2 us (level)
  no operation moved by 1% of the time
where the time goes in v8:
time: 92.2 us; the launch traced here: 92 us
  Pallas kernels  90.3 us (98%)
  local copies, waits for them, and re-layouts  1.69 us (2%)
    pallas_call x1, Pallas kernels, local(): pl.pallas_call(kernel, out_shape=jax.ShapeDtypeStruct((m, w), BF16), in_s...  90.3 us

profile of v8, /device:TPU:1, one launch (start us, length us, event | category | flops | bytes accessed | tf_op | source)
XLA Modules:
  0.0 92.0 jit_solution(10590782932043859807)
XLA Ops:
  0.0 0.0 copy-start
  0.0 1.0 %copy-done = bf16[400,352]{1,0:T(8,128)(2,1)S(1)} copy-done((bf16[400,352]{1,0:T(8,128)(2,1)S(1)}, bf16[400,352]{1,0:T(8,128)(2,1)}, u32[]{:S(2)}) %copy-start) | copy-done | bytes 281624
  1.0 90.3 %newton_schulz.1 = bf16[400,352]{1,0:T(8,128)(2,1)S(1)} custom-call(bf16[400,352]{1,0:T(8,128)(2,1)S(1)} %copy-done), custom_call_target="tpu_custom_call" | custom-call | tf_op jit(solution)/shard_map/newton_schulz/pallas_call | solution.py:394
  91.3 0.7 copy.3
Async XLA Ops:
  0.0 1.0 %copy-start = (bf16[400,352]{1,0:T(8,128)(2,1)S(1)}, bf16[400,352]{1,0:T(8,128)(2,1)}, u32[]{:S(2)}) copy-start(bf16[400,352]{1,0:T(8,128)(2,1)} %x_hbm.1) | copy-start | bytes 844804

commit v9 on v8

--- a/solution.py
+++ b/solution.py
@@ -352,9 +352,14 @@
     update = None
     held = [z]
     for step in range(1, 5):
-        ring_step4(*pring, step)
         got = [zslots[-step], zslots[step]] if step < 4 else [zslots[4]]
-        hand_over(got)
+        if step < 4:
+            ring_step4(*pring, step)
+            hand_over(got)
+        else:
+            for right, n in ((1, 0), (0, 1), (1, 2), (0, 3)):
+                ring_hop(*pring, step, right, n)
+                send(p_row(got[0], n), p_row(got[0], n), pcs, pcr.at[got[0]], core)
         for s in held:
             update = term(s) if update is None else update + term(s)
         held = got

time: 92.2 us -> 92 us (level)
  no operation moved by 1% of the time
where the time goes in v9:
time: 92 us; the launch traced here: 91.9 us
  Pallas kernels  90.2 us (98%)
  local copies, waits for them, and re-layouts  1.69 us (2%)
    pallas_call x1, Pallas kernels, local(): pl.pallas_call(kernel, out_shape=jax.ShapeDtypeStruct((m, w), BF16), in_s...  90.2 us

profile of v9, /device:TPU:1, one launch (start us, length us, event | category | flops | bytes accessed | tf_op | source)
XLA Modules:
  0.0 91.9 jit_solution(15359741512039813970)
XLA Ops:
  0.0 0.0 copy-start
  0.0 1.0 %copy-done = bf16[400,352]{1,0:T(8,128)(2,1)S(1)} copy-done((bf16[400,352]{1,0:T(8,128)(2,1)S(1)}, bf16[400,352]{1,0:T(8,128)(2,1)}, u32[]{:S(2)}) %copy-start) | copy-done | bytes 281624
  1.0 90.2 %newton_schulz.1 = bf16[400,352]{1,0:T(8,128)(2,1)S(1)} custom-call(bf16[400,352]{1,0:T(8,128)(2,1)S(1)} %copy-done), custom_call_target="tpu_custom_call" | custom-call | tf_op jit(solution)/shard_map/newton_schulz/pallas_call | solution.py:399
  91.2 0.7 copy.3
Async XLA Ops:
  0.0 1.0 %copy-start = (bf16[400,352]{1,0:T(8,128)(2,1)S(1)}, bf16[400,352]{1,0:T(8,128)(2,1)}, u32[]{:S(2)}) copy-start(bf16[400,352]{1,0:T(8,128)(2,1)} %x_hbm.1) | copy-start | bytes 844804

commit v10 on v8

--- a/solution.py
+++ b/solution.py
@@ -14,7 +14,7 @@
 NZ, NY, NX = 8, 4, 4
 NB = 8
 EARLY = 4
-UP = 256
+UP = 224
 START = 7
 MESH = pl.DeviceIdType.MESH
 F32, BF16 = jnp.float32, jnp.bfloat16

time: 92.2 us -> 92 us (level)
  no operation moved by 1% of the time
where the time goes in v10:
time: 92 us; the launch traced here: 91.8 us
  Pallas kernels  90.1 us (98%)
  local copies, waits for them, and re-layouts  1.69 us (2%)
    pallas_call x1, Pallas kernels, local(): pl.pallas_call(kernel, out_shape=jax.ShapeDtypeStruct((m, w), BF16), in_s...  90.1 us

profile of v10, /device:TPU:1, one launch (start us, length us, event | category | flops | bytes accessed | tf_op | source)
XLA Modules:
  0.0 91.8 jit_solution(6348617715273753602)
XLA Ops:
  0.0 0.0 copy-start
  0.0 1.0 %copy-done = bf16[400,352]{1,0:T(8,128)(2,1)S(1)} copy-done((bf16[400,352]{1,0:T(8,128)(2,1)S(1)}, bf16[400,352]{1,0:T(8,128)(2,1)}, u32[]{:S(2)}) %copy-start) | copy-done | bytes 281624
  1.0 90.1 %newton_schulz.1 = bf16[400,352]{1,0:T(8,128)(2,1)S(1)} custom-call(bf16[400,352]{1,0:T(8,128)(2,1)S(1)} %copy-done), custom_call_target="tpu_custom_call" | custom-call | tf_op jit(solution)/shard_map/newton_schulz/pallas_call | solution.py:394
  91.1 0.7 copy.3
Async XLA Ops:
  0.0 1.0 %copy-start = (bf16[400,352]{1,0:T(8,128)(2,1)S(1)}, bf16[400,352]{1,0:T(8,128)(2,1)}, u32[]{:S(2)}) copy-start(bf16[400,352]{1,0:T(8,128)(2,1)} %x_hbm.1) | copy-start | bytes 844804
